TPU v7x, 32 devices: a whole 2x2x4 slice. The times are simulated.
32 devices in a mesh: group: 2 (over x), frame: 16 (over z, y, core).
Axes of the slice: x: 2, y: 2, z: 4, core: 2. Of those that a mesh axis runs over, the one named last changes fastest.
Arguments:
- inputs: bfloat16 [12288, 1024], P(('group', 'frame')), parts along dimension 0, may hold values from -40 to 40
- grads_out: bfloat16 [12288, 1024], P(('group', 'frame')), parts along dimension 0, may hold values from -40 to 40
- owners: int32 [8], P('group'), parts along dimension 0, may hold values from 0 to 3, each once
Outputs:
- precond: bfloat16 [8, 512, 512], P('group'), parts along dimension 0
- roots: float32 [8192, 512], P(('group', 'frame')), parts along dimension 0
There are 2 independent parts, one for each index of `group`. A program takes and returns all parts, laid end to end along the dimension named above; each array names one. Nothing has to cross between parts.
Inputs may be any that keep to these rules, and one draw needn't show every extreme that they name: `owners`: each slot is named by exactly one block.
All inputs are finite; a program needn't handle non-finite values.
Results may differ from a plain program's by a relative error of at most 0.001.
Values may be sent and summed in bfloat16 or wider, within the bound.
A program may use at most 128 MiB of HBM per device.

v0:
```python
import jax
import jax.numpy as jnp
from jax import lax
from jax.sharding import PartitionSpec as P

BLOCK = 512
ITERS = 3


damping = 0.1


def partner_2(value, axis, stride):
    mask = 2**stride
    pairs = [(source, source ^ mask) for source in range(lax.axis_size(axis))]
    return lax.ppermute(value, axis, pairs)


def exact_dot(first_op, second_op):
    return jnp.dot(
        first_op, second_op, precision=lax.Precision.HIGHEST, preferred_element_type=jnp.float32
    )


def joined(own_part, other_part, own_first):
    return jnp.where(
        own_first,
        jnp.concatenate([own_part, other_part], 0),
        jnp.concatenate([other_part, own_part], 0),
    )


def body(inputs, grads_out, owners):
    frames = lax.axis_size("frame")
    blocks = frames // 4
    block_width = BLOCK
    quarter = block_width // 4
    half_rows = block_width // 2
    device_index = lax.axis_index("frame")
    quad_role = device_index % 4
    factor_side = quad_role // 2
    half_side = quad_role % 2
    token_scale = (inputs.shape[0] * frames) ** (-0.5)
    positions = jnp.arange(blocks, dtype=jnp.int32)
    inverse = jnp.sum(
        jnp.where(owners[None, :] == positions[:, None], positions[None, :], 0), axis=1
    )

    def block_product(block_id, row_offset, row_count):
        x_cols = lax.dynamic_slice_in_dim(
            inputs, block_id % 2 * block_width + row_offset, row_count, 1
        )
        y_cols = lax.dynamic_slice_in_dim(grads_out, block_id // 2 * block_width, block_width, 1)
        return (
            jnp.einsum("tk,tc->kc", x_cols, y_cols, preferred_element_type=jnp.float32)
            * token_scale
        )

    def one_slot(offset):
        return block_product(inverse[offset], 0, block_width)

    stacked = lax.map(
        one_slot, jnp.arange(lax.axis_size("frame") * quarter // block_width, dtype=jnp.int32)
    )
    own_part = lax.psum_scatter(
        stacked.reshape(lax.axis_size("frame") * quarter, block_width),
        "frame",
        scatter_dimension=0,
        tiled=True,
    )
    partner = partner_2(own_part, "frame", 0)
    pair_rows = joined(own_part, partner, half_side == 0)
    across = partner_2(pair_rows, "frame", 1)
    gradient = joined(pair_rows, across, factor_side == 0)
    operand = jnp.where(factor_side == 0, gradient, gradient.T)
    statistic = exact_dot(operand, operand.T) / block_width
    identity = jnp.eye(block_width, dtype=jnp.float32)
    damped = statistic + damping * jnp.trace(statistic) / block_width * identity
    frob_norm = jnp.sqrt(jnp.sum(damped * damped))
    zeta_scale = 5.0 / (2.0 * frob_norm)
    matrix = zeta_scale * damped
    root_full = zeta_scale**0.25 * identity
    for iteration in range(ITERS):
        factor_step = (5.0 * identity - matrix) * 0.25
        root_full = exact_dot(root_full, factor_step)
        square = exact_dot(factor_step, factor_step)
        matrix = exact_dot(exact_dot(square, square), matrix)
    roots_rows = lax.dynamic_slice_in_dim(root_full, half_side * half_rows, half_rows, 0)
    root_peer = partner_2(root_full, "frame", 1)
    left_root = jnp.where(factor_side == 0, root_full, root_peer)
    right_root = jnp.where(factor_side == 0, root_peer, root_full)
    left_rows = lax.dynamic_slice_in_dim(left_root, quad_role * quarter, quarter, 0)
    precond_rows = exact_dot(exact_dot(left_rows, gradient), right_root).astype(jnp.bfloat16)
    gathered = lax.all_gather(precond_rows, "frame", axis=0, tiled=True)
    gathered = gathered.reshape(blocks, block_width, block_width)
    precond = jnp.take(gathered, owners, axis=0)
    return (precond, roots_rows)


def solution(mesh):
    in_specs = (P(("group", "frame"), None), P(("group", "frame"), None), P("group"))
    out_specs = (P("group", None, None), P(("group", "frame"), None))
    return jax.shard_map(body, mesh=mesh, in_specs=in_specs, out_specs=out_specs, check_vma=False)
```

profile of v0, /device:TPU:1, one launch (start us, length us, event | category | flops | bytes accessed | tf_op | source)
XLA Modules:
  0.0 239.8 jit_solution(6445313658121730988)
XLA Ops:
  7.2 0.0 reduce-scatter.2.cloned.1.call-start
  7.2 0.8 select_reduce_fusion.1
  8.0 33.3 %while.12 = (s32[]{:T(128)}, f32[4,512,512]{2,1,0:T(8,128)}, s32[4]{0:T(128)S(1)}, s32[4]{0:T(128)S(1)}, bf16[384,1024]{1,0:T(8,128)(2,1)}, /*index=5*/bf16[384,...) while((s32[]{:T(128)}, f32[4,512,512]{2,1,0:T(8,128)}, ...), condition=%wide.region_2.3_spmd, body=%wide.region_1.2_spmd.sunk | while | flops 201588768 | bytes 1835490 | solution.py:62
  8.0 0.6 dynamic_slice.52
  10.5 0.6 dynamic_slice.53
  13.7 2.6 %fusion.74 = f32[4,512,512]{2,1,0:T(8,128)} fusion(f32[4,512,512]{2,1,0:T(8,128)} %get-tuple-element.148, s32[]{:T(128)S(6)} %copy.18, bf16[384,1024]{1,0:T(8,128)(2,1)} %get-tuple-element.165, s32[]{:T(128)S(6)} %select_n.161, bf16[384,1024]{1,0:T(8,128)(2,1)} %get-tuple-element.164, s32[]{:T(128)S(6)} %select_n.163), kind=kOutput, calls=%fused_computation.3.clone.1 | convolution fusion | flops 201588736 | bytes 1835020 | tf_op jit(solution)/shard_map/while/body/eval_jaxpr/tk,tc->kc/dot_general | solution.py:55
  16.3 0.6 dynamic_slice.52
  18.8 0.6 dynamic_slice.53
  22.0 2.6 %fusion.74 = f32[4,512,512]{2,1,0:T(8,128)} fusion(f32[4,512,512]{2,1,0:T(8,128)} %get-tuple-element.148, s32[]{:T(128)S(6)} %copy.18, bf16[384,1024]{1,0:T(8,128)(2,1)} %get-tuple-element.165, s32[]{:T(128)S(6)} %select_n.161, bf16[384,1024]{1,0:T(8,128)(2,1)} %get-tuple-element.164, s32[]{:T(128)S(6)} %select_n.163), kind=kOutput, calls=%fused_computation.3.clone.1 | convolution fusion | flops 201588736 | bytes 1835020 | tf_op jit(solution)/shard_map/while/body/eval_jaxpr/tk,tc->kc/dot_general | solution.py:55
  24.6 0.6 dynamic_slice.52
  27.2 0.6 dynamic_slice.53
  30.4 2.6 %fusion.74 = f32[4,512,512]{2,1,0:T(8,128)} fusion(f32[4,512,512]{2,1,0:T(8,128)} %get-tuple-element.148, s32[]{:T(128)S(6)} %copy.18, bf16[384,1024]{1,0:T(8,128)(2,1)} %get-tuple-element.165, s32[]{:T(128)S(6)} %select_n.161, bf16[384,1024]{1,0:T(8,128)(2,1)} %get-tuple-element.164, s32[]{:T(128)S(6)} %select_n.163), kind=kOutput, calls=%fused_computation.3.clone.1 | convolution fusion | flops 201588736 | bytes 1835020 | tf_op jit(solution)/shard_map/while/body/eval_jaxpr/tk,tc->kc/dot_general | solution.py:55
  32.9 0.6 dynamic_slice.52
  35.5 0.6 dynamic_slice.53
  38.7 2.6 %fusion.74 = f32[4,512,512]{2,1,0:T(8,128)} fusion(f32[4,512,512]{2,1,0:T(8,128)} %get-tuple-element.148, s32[]{:T(128)S(6)} %copy.18, bf16[384,1024]{1,0:T(8,128)(2,1)} %get-tuple-element.165, s32[]{:T(128)S(6)} %select_n.161, bf16[384,1024]{1,0:T(8,128)(2,1)} %get-tuple-element.164, s32[]{:T(128)S(6)} %select_n.163), kind=kOutput, calls=%fused_computation.3.clone.1 | convolution fusion | flops 201588736 | bytes 1835020 | tf_op jit(solution)/shard_map/while/body/eval_jaxpr/tk,tc->kc/dot_general | solution.py:55
  41.3 5.4 %copy.14 = f32[2048,512]{0,1:T(8,128)} copy(f32[2048,512]{1,0:T(8,128)} %bitcast.30) | data formatting | bytes 8388608 | tf_op jit(solution)/shard_map/reshape | solution.py:66
  46.7 0.0 reduce-scatter.2.cloned.1.call-update
  46.7 0.0 all-gather.2.cloned.1.call-start
  46.7 73.2 %reduce-scatter.2.cloned.1.call-done = f32[128,512]{0,1:T(8,128)} async-done(((f32[2048,512]{0,1:T(8,128)}), f32[128,512]{0,1:T(8,128)}) %reduce-scatter.2.cloned.1.call-update) | async-done | bytes 262160 | tf_op jit(solution)/shard_map/reduce_scatter | solution.py:65
  119.9 2.4 collective-permute-start
  122.3 1.4 collective-permute-done
  123.7 1.1 maximum_select_fusion.1
  124.7 0.5 collective-permute-start.1
  125.2 12.7 %collective-permute-done.1 = f32[256,512]{0,1:T(8,128)S(1)} collective-permute-done((f32[256,512]{0,1:T(8,128)S(1)}, f32[256,512]{0,1:T(8,128)S(1)}, u32[]{:S(2)}, u32[]{:S(2)}) %collective-permute-start.1) | collective-permute-done | bytes 524320 | tf_op jit(solution)/shard_map/ppermute | solution.py:16
  137.9 0.2 maximum_select_fusion
  138.1 0.3 copy.13
  138.5 2.6 %select_reduce_fusion = (f32[]{:T(128)}, f32[512,512]{1,0:T(8,128)S(1)}) fusion(f32[512,512]{1,0:T(8,128)S(1)} %copy.13, pred[]{:T(512)S(6)} %eq.43, f32[256,512]{0,1:T(8,128)S(1)} %maximum_select_fusion.1, f32[256,512]{0,1:T(8,128)S(1)} %collective-permute-done.1), kind=kOutput, calls=%fused_computation.23 | convolution fusion | flops 1612709888 | bytes 3145733 | tf_op jit(solution)/shard_map/dot_general | solution.py:20
  141.7 0.9 multiply_reduce_fusion
  143.3 2.0 fusion.17
  145.3 1.9 fusion.9
  147.2 1.8 fusion.55
  149.1 1.9 fusion.11
  151.0 1.9 fusion.13
  152.9 2.1 fusion.15
  155.0 1.8 fusion.56
  156.9 1.8 fusion.5
  158.7 1.8 fusion.57
  160.6 0.5 collective-permute-start.2
  161.1 0.0 copy-start
  161.1 23.0 %collective-permute-done.2 = f32[512,512]{1,0:T(8,128)S(1)} collective-permute-done((f32[512,512]{1,0:T(8,128)S(1)}, f32[512,512]{1,0:T(8,128)S(1)}, u32[]{:S(2)}, u32[]{:S(2)}) %collective-permute-start.2) | collective-permute-done | bytes 1048608 | tf_op jit(solution)/shard_map/ppermute | solution.py:16
  184.1 1.2 fusion.38
  185.3 1.4 convolution_convert_fusion
  186.7 0.0 all-gather.2.cloned.1.call-update
  186.7 0.0 copy-done
  186.8 0.8 constant_dynamic-slice_fusion
  187.6 41.6 %all-gather.2.cloned.1.call-done = bf16[2048,512]{1,0:T(8,128)(2,1)} async-done(((bf16[128,512]{1,0:T(8,128)(2,1)}), bf16[2048,512]{1,0:T(8,128)(2,1)}) %all-gather.2.cloned.1.call-update) | async-done | bytes 2097168 | tf_op jit(solution)/shard_map/all_gather | solution.py:94
  229.1 2.3 gather_fusion
  231.4 1.6 broadcast_select_fusion
  (5 shorter events, 0.0 us)
Async XLA Ops:
  7.2 112.7 %reduce-scatter.2.cloned.1.call-start = ((), (), s32[]{:S(2)}) async-start(), calls=%async_computation.1 | async-start | bytes 4456448 | tf_op jit(solution)/shard_map/reduce_scatter | solution.py:65
  46.7 182.5 %all-gather.2.cloned.1.call-start = ((), (), s32[]{:S(2)}) async-start(), calls=%async_computation.2 | async-start | bytes 2228224 | tf_op jit(solution)/shard_map/all_gather | solution.py:94
  119.9 3.8 %collective-permute-start = (f32[128,512]{0,1:T(8,128)}, f32[128,512]{0,1:T(8,128)S(1)}, u32[]{:S(2)}, u32[]{:S(2)}) collective-permute-start(f32[128,512]{0,1:T(8,128)} %reduce-scatter.2.cloned.1.call-done), channel_id=1, source_target_pairs={{0,1},{1,0},{2,3},{3,2},{4,5},{5,4},{6,7},{7,6},{8,9},{9,8},{10,11... | collective-permute-start | bytes 786440 | tf_op jit(solution)/shard_map/ppermute | solution.py:16
  124.7 13.2 %collective-permute-start.1 = (f32[256,512]{0,1:T(8,128)S(1)}, f32[256,512]{0,1:T(8,128)S(1)}, u32[]{:S(2)}, u32[]{:S(2)}) collective-permute-start(f32[256,512]{0,1:T(8,128)S(1)} %maximum_select_fusion.1), channel_id=1, source_target_pairs={{0,2},{1,3},{2,0},{3,1},{4,6},{5,7},{6,4},{7,5},{8,10},{9,11},{10,... | collective-permute-start | bytes 1572872 | tf_op jit(solution)/shard_map/ppermute | solution.py:16
  160.6 23.5 %collective-permute-start.2 = (f32[512,512]{1,0:T(8,128)S(1)}, f32[512,512]{1,0:T(8,128)S(1)}, u32[]{:S(2)}, u32[]{:S(2)}) collective-permute-start(f32[512,512]{1,0:T(8,128)S(1)} %fusion.57), channel_id=1, source_target_pairs={{0,2},{1,3},{2,0},{3,1},{4,6},{5,7},{6,4},{7,5},{8,10},{9,11},{10,... | collective-permute-start | bytes 3145736 | tf_op jit(solution)/shard_map/ppermute | solution.py:16
  161.1 25.6 %copy-start = (s32[4]{0:T(128)S(1)}, s32[4]{0:T(128)}, u32[]{:S(2)}) copy-start(s32[4]{0:T(128)} %param.7) | copy-start | bytes 52
Sparse Core Ops, SparseCore 0:
  46.8 73.0 reduce-scatter.1
  186.8 42.2 all-gather.1
where the time goes:
time: 241 us; the launch traced here: 240 us
  waiting for transfers between devices  152 us (63%)
  matrix products  32.6 us (14%)
  loops' own time  18.3 us (8%)
  between operations  15.6 us (6%)
  local copies, waits for them, and re-layouts  13.5 us (6%)
  other arithmetic  4.49 us (2%)
  starting transfers between devices  3.43 us (1%)
    reduce_scatter x1, waiting for transfers between devices, body(): lax.psum_scatter(stacked.reshape(lax.axis_size('frame') * quarter, block_...  73.2 us
    all_gather x1, waiting for transfers between devices, body(): gathered = lax.all_gather(precond_rows, 'frame', axis=0, tiled=True)  41.6 us
    ppermute x3, waiting for transfers between devices, partner_2(): return lax.ppermute(value, axis, pairs)  37.1 us
    dot_general x12, matrix products, exact_dot(): jnp.dot(first_op, second_op, precision=lax.Precision.HIGHEST, preferred_e...  22.3 us
    another operation x1, loops' own time, body(): lax.map(one_slot, jnp.arange(lax.axis_size('frame') * quarter // block_wi...  18.3 us
    dot_general x4, matrix products, block_product(): jnp.einsum('tk,tc->kc', x_cols, y_cols, preferred_element_type=jnp.float32)  10.3 us
    reshape x1, local copies, waits for them, and re-layouts, body(): stacked.reshape(lax.axis_size('frame') * quarter, block_width)  5.4 us
  transfers between devices with their start and end apart: 5, of which 5 were waited for; matrix products, arithmetic and copies ran while one was open for 0% of the time, Pallas kernels for 0%

commit v1 on v0

--- a/solution.py
+++ b/solution.py
@@ -1,6 +1,10 @@
+import functools
+
 import jax
 import jax.numpy as jnp
 from jax import lax
+from jax.experimental import pallas as pl
+from jax.experimental.pallas import tpu as pltpu
 from jax.sharding import PartitionSpec as P
 
 BLOCK = 512
@@ -30,7 +34,7 @@
     )
 
 
-def body(inputs, grads_out, owners):
+def body_general(inputs, grads_out, owners):
     frames = lax.axis_size("frame")
     blocks = frames // 4
     block_width = BLOCK
@@ -97,7 +101,231 @@
     return (precond, roots_rows)
 
 
+def halves(value):
+    high = value.astype(jnp.bfloat16)
+    low = (value - high.astype(jnp.float32)).astype(jnp.bfloat16)
+    return high, low
+
+
+def dot_halves(first, second, dims=((1,), (0,))):
+    def one(a, b):
+        return lax.dot_general(a, b, (dims, ((), ())), preferred_element_type=jnp.float32)
+
+    return one(first[0], second[0]) + (one(first[0], second[1]) + one(first[1], second[0]))
+
+
+def inverse_root(operand):
+    size = operand.shape[0]
+    parts = halves(operand)
+    statistic = dot_halves(parts, parts, ((1,), (1,))) / size
+    row = lax.broadcasted_iota(jnp.int32, (size, size), 0)
+    col = lax.broadcasted_iota(jnp.int32, (size, size), 1)
+    diagonal = row == col
+    trace = jnp.sum(jnp.where(diagonal, statistic, 0.0))
+    damped = statistic + jnp.where(diagonal, damping * trace / size, 0.0)
+    zeta = 5.0 / (2.0 * jnp.sqrt(jnp.full((1, 1), jnp.sum(damped * damped), jnp.float32)))
+    matrix = zeta * damped
+    a = 1.25
+    scale = 1.0
+    deviation = None
+    for iteration in range(ITERS):
+        step = matrix * -0.25
+        step_parts = halves(step)
+        if deviation is None:
+            deviation, scale = step, a
+        else:
+            deviation = scale * step + a * deviation + dot_halves(halves(deviation), step_parts)
+            scale = scale * a
+        if iteration < ITERS - 1:
+            square = 2.0 * a * step + dot_halves(step_parts, step_parts)
+            square_parts = halves(square)
+            fourth = 2.0 * a * a * square + dot_halves(square_parts, square_parts)
+            matrix = a**4 * matrix + dot_halves(halves(fourth), halves(matrix))
+    root_scale = jnp.sqrt(jnp.sqrt(zeta))
+    return root_scale * (deviation + jnp.where(diagonal, scale, 0.0))
+
+
+def kernel(
+    token_scale, owners_ref, x_ref, y_ref, out_ref, roots_ref,
+    xt, part, from_core, y_sum, from_y, z_sum, from_z, grad, root_own, root_peer, rows_all,
+    send_sem, recv_sem,
+):
+    me = lax.axis_index("frame")
+    z, role = me // 4, me % 4
+    y, core = role // 2, role % 2
+    core_peer = me + 1 - 2 * core
+    y_peer = me + 2 - 4 * y
+    role_y = role + 2 - 4 * y
+    planes = [((z + d) % 4) * 4 + role for d in range(4)]
+    quarter, width = grad.shape[1], grad.shape[2]
+    copies = []
+
+    def copy(src, dst, target):
+        index = len(copies)
+        made = pltpu.make_async_remote_copy(
+            src_ref=src,
+            dst_ref=dst,
+            send_sem=send_sem.at[index],
+            recv_sem=recv_sem.at[index],
+            device_id={"frame": target},
+            device_id_type=pl.DeviceIdType.MESH,
+        )
+        made.start()
+        copies.append(made)
+        return made
+
+    barrier = pltpu.get_barrier_semaphore()
+    partners = [core_peer, y_peer] + planes[1:]
+    for partner in partners:
+        pl.semaphore_signal(
+            barrier, inc=1, device_id={"frame": partner}, device_id_type=pl.DeviceIdType.MESH
+        )
+
+    xt[...] = x_ref[...].T
+
+    def compute(d):
+        slot = (z + d) % 4
+        row_bit, col_bit = jnp.int32(0), jnp.int32(0)
+        for b in range(1, 4):
+            here = (owners_ref[b] == slot).astype(jnp.int32)
+            row_bit, col_bit = row_bit + here * (b % 2), col_bit + here * (b // 2)
+        x_rows = jnp.where(
+            jnp.full((width, x_ref.shape[0]), row_bit) == 0, xt[:width, :], xt[width:, :]
+        )
+        y_cols = jnp.where(
+            jnp.full((x_ref.shape[0], width), col_bit) == 0, y_ref[:, :width], y_ref[:, width:]
+        )
+        part[d] = jnp.dot(x_rows, y_cols, preferred_element_type=jnp.float32).reshape(
+            4, quarter, width
+        )
+
+    def to_core(d):
+        return [
+            copy(
+                part.at[d, 2 * side + 1 - core], from_core.at[d, index], core_peer
+            )
+            for index, side in enumerate((1 - y, y))
+        ]
+
+    def to_y(d, sent):
+        sent[0].wait_recv()
+        y_sum[d] = part[d, 2 * (1 - y) + core] + from_core[d, 0]
+        return copy(y_sum.at[d], from_y.at[d], y_peer)
+
+    order = (2, 1, 3, 0)
+    core_copies, y_copies, z_copies = {}, {}, {}
+    for index, d in enumerate(order):
+        compute(d)
+        if index == 0:
+            pl.semaphore_wait(barrier, len(partners))
+        core_copies[d] = to_core(d)
+        if index > 0:
+            before = order[index - 1]
+            y_copies[before] = to_y(before, core_copies[before])
+    y_copies[0] = to_y(0, core_copies[0])
+    for d in order:
+        core_copies[d][1].wait_recv()
+        y_copies[d].wait_recv()
+        z_sum[d] = part[d, role] + from_core[d, 1] + from_y[d]
+        if d > 0:
+            z_copies[d] = copy(z_sum.at[d], from_z.at[d - 1], planes[d])
+    total = z_sum[0]
+    for d in order[:3]:
+        z_copies[d].wait_recv()
+        total = total + from_z[d - 1]
+    grad[role] = total * token_scale
+    own_core = copy(grad.at[role], grad.at[role], core_peer)
+    own_y = copy(grad.at[role], grad.at[role], y_peer)
+    own_y.wait_recv()
+    forward = copy(grad.at[role_y], grad.at[role_y], core_peer)
+    own_core.wait_recv()
+    forward.wait_recv()
+
+    gradient = grad[...].reshape(4 * quarter, width)
+    root_own[...] = inverse_root(jnp.where(core == 0, gradient, gradient.T))
+    exchange = copy(root_own, root_peer, core_peer)
+    exchange.wait_recv()
+
+    half = pl.ds(pl.multiple_of(core * 2 * quarter, 2 * quarter), 2 * quarter)
+    roots_ref[...] = jnp.where(y == core, root_own[half, :], root_peer[half, :])
+    mine = pl.ds(pl.multiple_of(role * quarter, quarter), quarter)
+    left = jnp.where(core == 0, root_own[mine, :], root_peer[mine, :])
+    right = jnp.where(core == 0, root_peer[...], root_own[...])
+    product = dot_halves(halves(left), halves(grad[...].reshape(4 * quarter, width)))
+    rows_all[z, role] = dot_halves(halves(product), halves(right)).astype(jnp.bfloat16)
+
+    def spread(plane, which, target):
+        place = rows_all.at[plane, which]
+        return copy(place, place, target)
+
+    z_rows = {d: spread(z, role, planes[d]) for d in (2, 1, 3)}
+    y_rows = {0: spread(z, role, y_peer)}
+    core_rows = [spread(z, role, core_peer)]
+    for d in (1, 3, 2):
+        z_rows[d].wait_recv()
+        plane = (z + 4 - d) % 4
+        y_rows[d] = spread(plane, role, y_peer)
+        core_rows.append(spread(plane, role, core_peer))
+    for d in (0, 1, 3, 2):
+        y_rows[d].wait_recv()
+        core_rows.append(spread((z + 4 - d) % 4, role_y, core_peer))
+    for made in core_rows:
+        made.wait_recv()
+    for b in range(4):
+        out_ref[b] = rows_all[owners_ref[b]].reshape(4 * quarter, width)
+    for made in copies:
+        made.wait_send()
+
+
+def body(inputs, grads_out, owners):
+    frames = lax.axis_size("frame")
+    quarter = BLOCK // 4
+    messages = 8 + 4 + 3 + 3 + 1 + 3 + 4 + 4 + 4
+    f32 = jnp.float32
+    return pl.pallas_call(
+        functools.partial(kernel, (inputs.shape[0] * frames) ** (-0.5)),
+        out_shape=(
+            jax.ShapeDtypeStruct((4, BLOCK, BLOCK), jnp.bfloat16),
+            jax.ShapeDtypeStruct((2 * quarter, BLOCK), f32),
+        ),
+        in_specs=[
+            pl.BlockSpec(memory_space=pltpu.SMEM),
+            pl.BlockSpec(memory_space=pltpu.VMEM),
+            pl.BlockSpec(memory_space=pltpu.VMEM),
+        ],
+        out_specs=(
+            pl.BlockSpec(memory_space=pltpu.VMEM),
+            pl.BlockSpec(memory_space=pltpu.VMEM),
+        ),
+        scratch_shapes=[
+            pltpu.VMEM((inputs.shape[1], inputs.shape[0]), jnp.bfloat16),
+            pltpu.VMEM((4, 4, quarter, BLOCK), f32),
+            pltpu.VMEM((4, 2, quarter, BLOCK), f32),
+            pltpu.VMEM((4, quarter, BLOCK), f32),
+            pltpu.VMEM((4, quarter, BLOCK), f32),
+            pltpu.VMEM((4, quarter, BLOCK), f32),
+            pltpu.VMEM((3, quarter, BLOCK), f32),
+            pltpu.VMEM((4, quarter, BLOCK), f32),
+            pltpu.VMEM((BLOCK, BLOCK), f32),
+            pltpu.VMEM((BLOCK, BLOCK), f32),
+            pltpu.VMEM((4, 4, quarter, BLOCK), jnp.bfloat16),
+            pltpu.SemaphoreType.DMA((messages,)),
+            pltpu.SemaphoreType.DMA((messages,)),
+        ],
+        compiler_params=pltpu.CompilerParams(
+            collective_id=0, has_side_effects=True, vmem_limit_bytes=56 * 2**20
+        ),
+    )(owners, inputs, grads_out)
+
+
 def solution(mesh):
     in_specs = (P(("group", "frame"), None), P(("group", "frame"), None), P("group"))
     out_specs = (P("group", None, None), P(("group", "frame"), None))
-    return jax.shard_map(body, mesh=mesh, in_specs=in_specs, out_specs=out_specs, check_vma=False)
+    fused = mesh.shape["frame"] == 16
+    return jax.shard_map(
+        body if fused else body_general,
+        mesh=mesh,
+        in_specs=in_specs,
+        out_specs=out_specs,
+        check_vma=False,
+    )

time: 241 us -> 88.7 us (0.37)
  the two profiles are of different devices: /device:TPU:1 before, /device:TPU:17 now
where the time goes in v1:
time: 88.7 us; the launch traced here: 88.5 us
  Pallas kernels  84 us (95%)
  local copies, waits for them, and re-layouts  3.9 us (4%)
    pallas_call x1, Pallas kernels, body(): pl.pallas_call(functools.partial(kernel, (inputs.shape[0] * frames) ** (-...  84 us
    unnamed x4, local copies, waits for them, and re-layouts  3.9 us

profile of v1, /device:TPU:17, one launch (start us, length us, event | category | flops | bytes accessed | tf_op | source)
XLA Modules:
  0.0 88.5 jit_solution(17664070572468736223)
XLA Ops:
  0.6 84.0 %shard_map.50 = (bf16[4,512,512]{2,1,0:T(8,128)(2,1)}, f32[256,512]{1,0:T(8,128)}) custom-call(s32[4]{0:T(128)} %owners_ref.1, bf16[384,1024]{1,0:T(8,128)(2,1)} %x_ref.1, bf16[384,1024]{1,0:T(8,128)(2,1)} %y_ref.1), custom_call_target="tpu_custom_call" | custom-call | tf_op jit(solution)/shard_map/pallas_call | solution.py:285
  84.6 0.0 copy-start
  84.6 3.1 %copy.7 = bf16[4,512,512]{2,1,0:T(8,128)(2,1)} copy(bf16[4,512,512]{2,1,0:T(8,128)(2,1)} %get-tuple-element.4) | data formatting | bytes 4194304
  87.7 0.0 copy-done
  87.8 0.8 copy.8
Async XLA Ops:
  84.6 3.1 %copy-start = (f32[256,512]{1,0:T(8,128)S(1)}, f32[256,512]{1,0:T(8,128)}, u32[]{:S(2)}) copy-start(f32[256,512]{1,0:T(8,128)} %get-tuple-element.5) | copy-start | bytes 1572868

commit v2 on v1

--- a/solution.py
+++ b/solution.py
@@ -181,50 +181,52 @@
             barrier, inc=1, device_id={"frame": partner}, device_id_type=pl.DeviceIdType.MESH
         )
 
-    xt[...] = x_ref[...].T
-
-    def compute(d):
+    half_width = width // 2
+    for side in (1 - y, y):
+        for bit in range(2):
+            cols = pl.ds(pl.multiple_of(bit * width + side * half_width, half_width), half_width)
+            xt[2 * bit + side] = x_ref[:, cols].T
+
+    def compute(d, side):
         slot = (z + d) % 4
         row_bit, col_bit = jnp.int32(0), jnp.int32(0)
         for b in range(1, 4):
             here = (owners_ref[b] == slot).astype(jnp.int32)
             row_bit, col_bit = row_bit + here * (b % 2), col_bit + here * (b // 2)
         x_rows = jnp.where(
-            jnp.full((width, x_ref.shape[0]), row_bit) == 0, xt[:width, :], xt[width:, :]
+            jnp.full((half_width, x_ref.shape[0]), row_bit) == 0, xt[side], xt[2 + side]
         )
         y_cols = jnp.where(
             jnp.full((x_ref.shape[0], width), col_bit) == 0, y_ref[:, :width], y_ref[:, width:]
         )
-        part[d] = jnp.dot(x_rows, y_cols, preferred_element_type=jnp.float32).reshape(
-            4, quarter, width
-        )
-
-    def to_core(d):
-        return [
-            copy(
-                part.at[d, 2 * side + 1 - core], from_core.at[d, index], core_peer
-            )
-            for index, side in enumerate((1 - y, y))
-        ]
+        product = jnp.dot(x_rows, y_cols, preferred_element_type=jnp.float32)
+        part[d, 2 * side] = product[:quarter]
+        part[d, 2 * side + 1] = product[quarter:]
+
+    def to_core(d, side, index):
+        return copy(part.at[d, 2 * side + 1 - core], from_core.at[d, index], core_peer)
 
     def to_y(d, sent):
-        sent[0].wait_recv()
+        sent.wait_recv()
         y_sum[d] = part[d, 2 * (1 - y) + core] + from_core[d, 0]
         return copy(y_sum.at[d], from_y.at[d], y_peer)
 
     order = (2, 1, 3, 0)
-    core_copies, y_copies, z_copies = {}, {}, {}
+    away, kept, y_copies, z_copies = {}, {}, {}, {}
     for index, d in enumerate(order):
-        compute(d)
+        compute(d, 1 - y)
         if index == 0:
             pl.semaphore_wait(barrier, len(partners))
-        core_copies[d] = to_core(d)
+        away[d] = to_core(d, 1 - y, 0)
         if index > 0:
             before = order[index - 1]
-            y_copies[before] = to_y(before, core_copies[before])
-    y_copies[0] = to_y(0, core_copies[0])
+            y_copies[before] = to_y(before, away[before])
+    y_copies[0] = to_y(0, away[0])
     for d in order:
-        core_copies[d][1].wait_recv()
+        compute(d, y)
+        kept[d] = to_core(d, y, 1)
+    for d in order:
+        kept[d].wait_recv()
         y_copies[d].wait_recv()
         z_sum[d] = part[d, role] + from_core[d, 1] + from_y[d]
         if d > 0:
@@ -254,33 +256,99 @@
     product = dot_halves(halves(left), halves(grad[...].reshape(4 * quarter, width)))
     rows_all[z, role] = dot_halves(halves(product), halves(right)).astype(jnp.bfloat16)
 
-    def spread(plane, which, target):
+    base = len(copies)
+    up, down, over, near, passed = base, base + 3, base + 6, base + 10, base + 14
+    above, below = planes[1], planes[3]
+
+    def rows_copy(index, plane, which, target):
         place = rows_all.at[plane, which]
-        return copy(place, place, target)
-
-    z_rows = {d: spread(z, role, planes[d]) for d in (2, 1, 3)}
-    y_rows = {0: spread(z, role, y_peer)}
-    core_rows = [spread(z, role, core_peer)]
-    for d in (1, 3, 2):
-        z_rows[d].wait_recv()
-        plane = (z + 4 - d) % 4
-        y_rows[d] = spread(plane, role, y_peer)
-        core_rows.append(spread(plane, role, core_peer))
-    for d in (0, 1, 3, 2):
-        y_rows[d].wait_recv()
-        core_rows.append(spread((z + 4 - d) % 4, role_y, core_peer))
-    for made in core_rows:
-        made.wait_recv()
+        return pltpu.make_async_remote_copy(
+            src_ref=place,
+            dst_ref=place,
+            send_sem=send_sem.at[index],
+            recv_sem=recv_sem.at[index],
+            device_id={"frame": target},
+            device_id_type=pl.DeviceIdType.MESH,
+        )
+
+    def share(plane):
+        rows_copy(over + plane, plane, role, y_peer).start()
+        rows_copy(near + plane, plane, role, core_peer).start()
+
+    def along(k):
+        @pl.when(z >= k)
+        def _():
+            rows_copy(up + k - 1, z - k, role, above).wait_recv()
+            if k < 3:
+                @pl.when(z < 3)
+                def _():
+                    rows_copy(up + k, z - k, role, above).start()
+            share(z - k)
+
+        @pl.when(z + k <= 3)
+        def _():
+            rows_copy(down + k - 1, z + k, role, below).wait_recv()
+            if k < 3:
+                @pl.when(z > 0)
+                def _():
+                    rows_copy(down + k, z + k, role, below).start()
+            share(z + k)
+
+    def pass_on(plane):
+        rows_copy(over + plane, plane, role, y_peer).wait_recv()
+        rows_copy(passed + plane, plane, role_y, core_peer).start()
+
+    def pass_step(k):
+        @pl.when(z >= k)
+        def _():
+            pass_on(z - k)
+
+        @pl.when(z + k <= 3)
+        def _():
+            pass_on(z + k)
+
+    @pl.when(z < 3)
+    def _():
+        rows_copy(up, z, role, above).start()
+
+    @pl.when(z > 0)
+    def _():
+        rows_copy(down, z, role, below).start()
+
+    share(z)
+    along(1)
+    pass_on(z)
+    along(2)
+    pass_step(1)
+    along(3)
+    pass_step(2)
+    pass_step(3)
+    for plane in range(4):
+        rows_copy(near + plane, plane, role, core_peer).wait_recv()
+        rows_copy(passed + plane, plane, role_y, core_peer).wait_recv()
     for b in range(4):
         out_ref[b] = rows_all[owners_ref[b]].reshape(4 * quarter, width)
     for made in copies:
         made.wait_send()
+    for k in range(3):
+        @pl.when((z >= k) & (z < 3))
+        def _():
+            rows_copy(up + k, z, role, above).wait_send()
+
+        @pl.when((z + k <= 3) & (z > 0))
+        def _():
+            rows_copy(down + k, z, role, below).wait_send()
+
+    for plane in range(4):
+        rows_copy(over + plane, plane, role, y_peer).wait_send()
+        rows_copy(near + plane, plane, role, core_peer).wait_send()
+        rows_copy(passed + plane, plane, role_y, core_peer).wait_send()
 
 
 def body(inputs, grads_out, owners):
     frames = lax.axis_size("frame")
     quarter = BLOCK // 4
-    messages = 8 + 4 + 3 + 3 + 1 + 3 + 4 + 4 + 4
+    messages = 8 + 4 + 3 + 3 + 1 + 3 + 3 + 4 + 4 + 4
     f32 = jnp.float32
     return pl.pallas_call(
         functools.partial(kernel, (inputs.shape[0] * frames) ** (-0.5)),
@@ -298,7 +366,7 @@
             pl.BlockSpec(memory_space=pltpu.VMEM),
         ),
         scratch_shapes=[
-            pltpu.VMEM((inputs.shape[1], inputs.shape[0]), jnp.bfloat16),
+            pltpu.VMEM((4, inputs.shape[1] // 4, inputs.shape[0]), jnp.bfloat16),
             pltpu.VMEM((4, 4, quarter, BLOCK), f32),
             pltpu.VMEM((4, 2, quarter, BLOCK), f32),
             pltpu.VMEM((4, quarter, BLOCK), f32),

time: 88.7 us -> 84.8 us (0.956)
  the two profiles are of different devices: /device:TPU:17 before, /device:TPU:1 now
where the time goes in v2:
time: 84.8 us; the launch traced here: 84.6 us
  Pallas kernels  80.1 us (94%)
  local copies, waits for them, and re-layouts  3.9 us (5%)
    pallas_call x1, Pallas kernels, body(): pl.pallas_call(functools.partial(kernel, (inputs.shape[0] * frames) ** (-...  80.1 us
    unnamed x4, local copies, waits for them, and re-layouts  3.9 us

profile of v2, /device:TPU:1, one launch (start us, length us, event | category | flops | bytes accessed | tf_op | source)
XLA Modules:
  0.0 84.6 jit_solution(2385132764226781421)
XLA Ops:
  0.6 80.1 %shard_map.50 = (bf16[4,512,512]{2,1,0:T(8,128)(2,1)}, f32[256,512]{1,0:T(8,128)}) custom-call(s32[4]{0:T(128)} %owners_ref.1, bf16[384,1024]{1,0:T(8,128)(2,1)} %x_ref.1, bf16[384,1024]{1,0:T(8,128)(2,1)} %y_ref.1), custom_call_target="tpu_custom_call" | custom-call | tf_op jit(solution)/shard_map/pallas_call | solution.py:353
  80.7 0.0 copy-start
  80.7 3.1 %copy.7 = bf16[4,512,512]{2,1,0:T(8,128)(2,1)} copy(bf16[4,512,512]{2,1,0:T(8,128)(2,1)} %get-tuple-element.4) | data formatting | bytes 4194304
  83.8 0.0 copy-done
  83.8 0.8 copy.8
Async XLA Ops:
  80.7 3.1 %copy-start = (f32[256,512]{1,0:T(8,128)S(1)}, f32[256,512]{1,0:T(8,128)}, u32[]{:S(2)}) copy-start(f32[256,512]{1,0:T(8,128)} %get-tuple-element.5) | copy-start | bytes 1572868

commit v3 on v2

--- a/solution.py
+++ b/solution.py
@@ -108,10 +108,9 @@
 
 
 def dot_halves(first, second, dims=((1,), (0,))):
-    def one(a, b):
-        return lax.dot_general(a, b, (dims, ((), ())), preferred_element_type=jnp.float32)
-
-    return one(first[0], second[0]) + (one(first[0], second[1]) + one(first[1], second[0]))
+    left = jnp.concatenate([first[0], first[1], first[0]], dims[0][0])
+    right = jnp.concatenate([second[0], second[0], second[1]], dims[1][0])
+    return lax.dot_general(left, right, (dims, ((), ())), preferred_element_type=jnp.float32)
 
 
 def inverse_root(operand):
@@ -222,15 +221,20 @@
             before = order[index - 1]
             y_copies[before] = to_y(before, away[before])
     y_copies[0] = to_y(0, away[0])
-    for d in order:
-        compute(d, y)
-        kept[d] = to_core(d, y, 1)
-    for d in order:
+
+    def to_z(d):
         kept[d].wait_recv()
         y_copies[d].wait_recv()
         z_sum[d] = part[d, role] + from_core[d, 1] + from_y[d]
         if d > 0:
             z_copies[d] = copy(z_sum.at[d], from_z.at[d - 1], planes[d])
+
+    for index, d in enumerate(order):
+        compute(d, y)
+        kept[d] = to_core(d, y, 1)
+        if index > 0:
+            to_z(order[index - 1])
+    to_z(0)
     total = z_sum[0]
     for d in order[:3]:
         z_copies[d].wait_recv()

time: 84.8 us -> 84.7 us (level)
  no operation moved by 1% of the time
where the time goes in v3:
time: 84.7 us; the launch traced here: 84.6 us
  Pallas kernels  80 us (94%)
  local copies, waits for them, and re-layouts  3.9 us (5%)
    pallas_call x1, Pallas kernels, body(): pl.pallas_call(functools.partial(kernel, (inputs.shape[0] * frames) ** (-...  80 us
    unnamed x4, local copies, waits for them, and re-layouts  3.9 us

profile of v3, /device:TPU:1, one launch (start us, length us, event | category | flops | bytes accessed | tf_op | source)
XLA Modules:
  0.0 84.6 jit_solution(11984901338781598021)
XLA Ops:
  0.6 80.0 %shard_map.50 = (bf16[4,512,512]{2,1,0:T(8,128)(2,1)}, f32[256,512]{1,0:T(8,128)}) custom-call(s32[4]{0:T(128)} %owners_ref.1, bf16[384,1024]{1,0:T(8,128)(2,1)} %x_ref.1, bf16[384,1024]{1,0:T(8,128)(2,1)} %y_ref.1), custom_call_target="tpu_custom_call" | custom-call | tf_op jit(solution)/shard_map/pallas_call | solution.py:357
  80.7 0.0 copy-start
  80.7 3.1 %copy.7 = bf16[4,512,512]{2,1,0:T(8,128)(2,1)} copy(bf16[4,512,512]{2,1,0:T(8,128)(2,1)} %get-tuple-element.4) | data formatting | bytes 4194304
  83.8 0.0 copy-done
  83.8 0.8 copy.8
Async XLA Ops:
  80.7 3.1 %copy-start = (f32[256,512]{1,0:T(8,128)S(1)}, f32[256,512]{1,0:T(8,128)}, u32[]{:S(2)}) copy-start(f32[256,512]{1,0:T(8,128)} %get-tuple-element.5) | copy-start | bytes 1572868

commit v4 on v2

--- a/solution.py
+++ b/solution.py
@@ -188,7 +188,7 @@
             xt[2 * bit + side] = x_ref[:, cols].T
 
     def compute(d, side):
-        slot = (z + d) % 4
+        slot = slots[d]
         row_bit, col_bit = jnp.int32(0), jnp.int32(0)
         for b in range(1, 4):
             here = (owners_ref[b] == slot).astype(jnp.int32)
@@ -211,8 +211,10 @@
         y_sum[d] = part[d, 2 * (1 - y) + core] + from_core[d, 0]
         return copy(y_sum.at[d], from_y.at[d], y_peer)
 
-    order = (2, 1, 3, 0)
-    away, kept, y_copies, z_copies = {}, {}, {}, {}
+    order = (0, 1, 2, 3)
+    first, third = 3 * (1 - z // 2), 1 + z % 2
+    slots = (first, 6 - first - third - z, third, z)
+    away, kept, y_copies = {}, {}, {}
     for index, d in enumerate(order):
         compute(d, 1 - y)
         if index == 0:
@@ -221,20 +223,48 @@
         if index > 0:
             before = order[index - 1]
             y_copies[before] = to_y(before, away[before])
-    y_copies[0] = to_y(0, away[0])
+    y_copies[3] = to_y(3, away[3])
     for d in order:
         compute(d, y)
         kept[d] = to_core(d, y, 1)
+    chain = send_sem.shape[0] - 8
+
+    def z_copy(d, way):
+        index = chain + 4 * way + slots[d]
+        return pltpu.make_async_remote_copy(
+            src_ref=z_sum.at[d],
+            dst_ref=from_z.at[way, slots[d]],
+            send_sem=send_sem.at[index],
+            recv_sem=recv_sem.at[index],
+            device_id={"frame": planes[1] if way == 0 else planes[3]},
+            device_id_type=pl.DeviceIdType.MESH,
+        )
+
+    def add_arrived(d, way):
+        @pl.when((z > 0) if way == 0 else (z < 3))
+        def _():
+            z_copy(d, way).wait_recv()
+            z_sum[d] = z_sum[d] + from_z[way, slots[d]]
+
     for d in order:
         kept[d].wait_recv()
         y_copies[d].wait_recv()
         z_sum[d] = part[d, role] + from_core[d, 1] + from_y[d]
-        if d > 0:
-            z_copies[d] = copy(z_sum.at[d], from_z.at[d - 1], planes[d])
-    total = z_sum[0]
-    for d in order[:3]:
-        z_copies[d].wait_recv()
-        total = total + from_z[d - 1]
+        if d < 3:
+            @pl.when(slots[d] > z)
+            def _():
+                add_arrived(d, 0)
+                z_copy(d, 0).start()
+
+            @pl.when(slots[d] < z)
+            def _():
+                add_arrived(d, 1)
+                z_copy(d, 1).start()
+
+        else:
+            add_arrived(d, 0)
+            add_arrived(d, 1)
+    total = z_sum[3]
     grad[role] = total * token_scale
     own_core = copy(grad.at[role], grad.at[role], core_peer)
     own_y = copy(grad.at[role], grad.at[role], y_peer)
@@ -330,6 +360,15 @@
         out_ref[b] = rows_all[owners_ref[b]].reshape(4 * quarter, width)
     for made in copies:
         made.wait_send()
+    for d in range(3):
+        @pl.when(slots[d] > z)
+        def _():
+            z_copy(d, 0).wait_send()
+
+        @pl.when(slots[d] < z)
+        def _():
+            z_copy(d, 1).wait_send()
+
     for k in range(3):
         @pl.when((z >= k) & (z < 3))
         def _():
@@ -348,7 +387,7 @@
 def body(inputs, grads_out, owners):
     frames = lax.axis_size("frame")
     quarter = BLOCK // 4
-    messages = 8 + 4 + 3 + 3 + 1 + 3 + 3 + 4 + 4 + 4
+    messages = 8 + 4 + 3 + 1 + 3 + 3 + 4 + 4 + 4 + 8
     f32 = jnp.float32
     return pl.pallas_call(
         functools.partial(kernel, (inputs.shape[0] * frames) ** (-0.5)),
@@ -372,7 +411,7 @@
             pltpu.VMEM((4, quarter, BLOCK), f32),
             pltpu.VMEM((4, quarter, BLOCK), f32),
             pltpu.VMEM((4, quarter, BLOCK), f32),
-            pltpu.VMEM((3, quarter, BLOCK), f32),
+            pltpu.VMEM((2, 4, quarter, BLOCK), f32),
             pltpu.VMEM((4, quarter, BLOCK), f32),
             pltpu.VMEM((BLOCK, BLOCK), f32),
             pltpu.VMEM((BLOCK, BLOCK), f32),

time: 84.8 us -> 83.4 us (0.983)
  Pallas kernels: 80.1 us -> 78.7 us
    pallas_call x1, Pallas kernels: 80.1 us -> 78.7 us  [body(): pl.pallas_call(functools.partial(kernel, (inputs.shape[0] * frames) ** (-...]
where the time goes in v4:
time: 83.4 us; the launch traced here: 83.2 us
  Pallas kernels  78.7 us (94%)
  local copies, waits for them, and re-layouts  3.9 us (5%)
    pallas_call x1, Pallas kernels, body(): pl.pallas_call(functools.partial(kernel, (inputs.shape[0] * frames) ** (-...  78.7 us
    unnamed x4, local copies, waits for them, and re-layouts  3.9 us

profile of v4, /device:TPU:1, one launch (start us, length us, event | category | flops | bytes accessed | tf_op | source)
XLA Modules:
  0.0 83.2 jit_solution(1271789458845683388)
XLA Ops:
  0.6 78.7 %shard_map.50 = (bf16[4,512,512]{2,1,0:T(8,128)(2,1)}, f32[256,512]{1,0:T(8,128)}) custom-call(s32[4]{0:T(128)} %owners_ref.1, bf16[384,1024]{1,0:T(8,128)(2,1)} %x_ref.1, bf16[384,1024]{1,0:T(8,128)(2,1)} %y_ref.1), custom_call_target="tpu_custom_call" | custom-call | tf_op jit(solution)/shard_map/pallas_call | solution.py:392
  79.3 0.0 copy-start
  79.3 3.1 %copy.7 = bf16[4,512,512]{2,1,0:T(8,128)(2,1)} copy(bf16[4,512,512]{2,1,0:T(8,128)(2,1)} %get-tuple-element.4) | data formatting | bytes 4194304
  82.4 0.0 copy-done
  82.4 0.8 copy.8
Async XLA Ops:
  79.3 3.1 %copy-start = (f32[256,512]{1,0:T(8,128)S(1)}, f32[256,512]{1,0:T(8,128)}, u32[]{:S(2)}) copy-start(f32[256,512]{1,0:T(8,128)} %get-tuple-element.5) | copy-start | bytes 1572868

commit v5 on v4

--- a/solution.py
+++ b/solution.py
@@ -182,10 +182,13 @@
         )
 
     half_width = width // 2
-    for side in (1 - y, y):
+
+    def turn(side):
         for bit in range(2):
             cols = pl.ds(pl.multiple_of(bit * width + side * half_width, half_width), half_width)
             xt[2 * bit + side] = x_ref[:, cols].T
+
+    turn(1 - y)
 
     def compute(d, side):
         slot = slots[d]
@@ -224,6 +227,7 @@
             before = order[index - 1]
             y_copies[before] = to_y(before, away[before])
     y_copies[3] = to_y(3, away[3])
+    turn(y)
     for d in order:
         compute(d, y)
         kept[d] = to_core(d, y, 1)
@@ -287,11 +291,13 @@
     rows_all[z, role] = dot_halves(halves(product), halves(right)).astype(jnp.bfloat16)
 
     base = len(copies)
+    piece = quarter // 2
     up, down, over, near, passed = base, base + 3, base + 6, base + 10, base + 14
     above, below = planes[1], planes[3]
 
-    def rows_copy(index, plane, which, target):
-        place = rows_all.at[plane, which]
+    def rows_copy(number, plane, which, target, h):
+        place = rows_all.at[plane, which, pl.ds(h * piece, piece)]
+        index = base + 2 * (number - base) + h
         return pltpu.make_async_remote_copy(
             src_ref=place,
             dst_ref=place,
@@ -301,61 +307,70 @@
             device_id_type=pl.DeviceIdType.MESH,
         )
 
-    def share(plane):
-        rows_copy(over + plane, plane, role, y_peer).start()
-        rows_copy(near + plane, plane, role, core_peer).start()
-
-    def along(k):
+    def share(plane, h):
+        rows_copy(over + plane, plane, role, y_peer, h).start()
+        rows_copy(near + plane, plane, role, core_peer, h).start()
+
+    def along(k, h):
         @pl.when(z >= k)
         def _():
-            rows_copy(up + k - 1, z - k, role, above).wait_recv()
+            rows_copy(up + k - 1, z - k, role, above, h).wait_recv()
             if k < 3:
                 @pl.when(z < 3)
                 def _():
-                    rows_copy(up + k, z - k, role, above).start()
-            share(z - k)
+                    rows_copy(up + k, z - k, role, above, h).start()
+            share(z - k, h)
 
         @pl.when(z + k <= 3)
         def _():
-            rows_copy(down + k - 1, z + k, role, below).wait_recv()
+            rows_copy(down + k - 1, z + k, role, below, h).wait_recv()
             if k < 3:
                 @pl.when(z > 0)
                 def _():
-                    rows_copy(down + k, z + k, role, below).start()
-            share(z + k)
-
-    def pass_on(plane):
-        rows_copy(over + plane, plane, role, y_peer).wait_recv()
-        rows_copy(passed + plane, plane, role_y, core_peer).start()
-
-    def pass_step(k):
+                    rows_copy(down + k, z + k, role, below, h).start()
+            share(z + k, h)
+
+    def pass_on(plane, h):
+        rows_copy(over + plane, plane, role, y_peer, h).wait_recv()
+        rows_copy(passed + plane, plane, role_y, core_peer, h).start()
+
+    def pass_step(k, h):
         @pl.when(z >= k)
         def _():
-            pass_on(z - k)
+            pass_on(z - k, h)
 
         @pl.when(z + k <= 3)
         def _():
-            pass_on(z + k)
-
-    @pl.when(z < 3)
-    def _():
-        rows_copy(up, z, role, above).start()
-
-    @pl.when(z > 0)
-    def _():
-        rows_copy(down, z, role, below).start()
-
-    share(z)
-    along(1)
-    pass_on(z)
-    along(2)
-    pass_step(1)
-    along(3)
-    pass_step(2)
-    pass_step(3)
+            pass_on(z + k, h)
+
+    def begin(h):
+        @pl.when(z < 3)
+        def _():
+            rows_copy(up, z, role, above, h).start()
+
+        @pl.when(z > 0)
+        def _():
+            rows_copy(down, z, role, below, h).start()
+
+        share(z, h)
+
+    both = range(2)
+    for h in both:
+        begin(h)
+    for h in both:
+        along(1, h)
+    for h in both:
+        pass_on(z, h)
+    for k in (2, 3):
+        for h in both:
+            along(k, h)
+            pass_step(k - 1, h)
+    for h in both:
+        pass_step(3, h)
     for plane in range(4):
-        rows_copy(near + plane, plane, role, core_peer).wait_recv()
-        rows_copy(passed + plane, plane, role_y, core_peer).wait_recv()
+        for h in both:
+            rows_copy(near + plane, plane, role, core_peer, h).wait_recv()
+            rows_copy(passed + plane, plane, role_y, core_peer, h).wait_recv()
     for b in range(4):
         out_ref[b] = rows_all[owners_ref[b]].reshape(4 * quarter, width)
     for made in copies:
@@ -369,25 +384,26 @@
         def _():
             z_copy(d, 1).wait_send()
 
-    for k in range(3):
-        @pl.when((z >= k) & (z < 3))
-        def _():
-            rows_copy(up + k, z, role, above).wait_send()
-
-        @pl.when((z + k <= 3) & (z > 0))
-        def _():
-            rows_copy(down + k, z, role, below).wait_send()
-
-    for plane in range(4):
-        rows_copy(over + plane, plane, role, y_peer).wait_send()
-        rows_copy(near + plane, plane, role, core_peer).wait_send()
-        rows_copy(passed + plane, plane, role_y, core_peer).wait_send()
+    for h in both:
+        for k in range(3):
+            @pl.when((z >= k) & (z < 3))
+            def _():
+                rows_copy(up + k, z, role, above, h).wait_send()
+
+            @pl.when((z + k <= 3) & (z > 0))
+            def _():
+                rows_copy(down + k, z, role, below, h).wait_send()
+
+        for plane in range(4):
+            rows_copy(over + plane, plane, role, y_peer, h).wait_send()
+            rows_copy(near + plane, plane, role, core_peer, h).wait_send()
+            rows_copy(passed + plane, plane, role_y, core_peer, h).wait_send()
 
 
 def body(inputs, grads_out, owners):
     frames = lax.axis_size("frame")
     quarter = BLOCK // 4
-    messages = 8 + 4 + 3 + 1 + 3 + 3 + 4 + 4 + 4 + 8
+    messages = 8 + 4 + 3 + 1 + 2 * (3 + 3 + 4 + 4 + 4) + 8
     f32 = jnp.float32
     return pl.pallas_call(
         functools.partial(kernel, (inputs.shape[0] * frames) ** (-0.5)),

time: 83.4 us -> 81.5 us (0.977)
  Pallas kernels: 78.7 us -> 76.8 us
    pallas_call x1, Pallas kernels: 78.7 us -> 76.8 us  [body(): pl.pallas_call(functools.partial(kernel, (inputs.shape[0] * frames) ** (-...]
where the time goes in v5:
time: 81.5 us; the launch traced here: 81.4 us
  Pallas kernels  76.8 us (94%)
  local copies, waits for them, and re-layouts  3.9 us (5%)
    pallas_call x1, Pallas kernels, body(): pl.pallas_call(functools.partial(kernel, (inputs.shape[0] * frames) ** (-...  76.8 us
    unnamed x4, local copies, waits for them, and re-layouts  3.9 us

profile of v5, /device:TPU:1, one launch (start us, length us, event | category | flops | bytes accessed | tf_op | source)
XLA Modules:
  0.0 81.4 jit_solution(7993220621798959625)
XLA Ops:
  0.6 76.8 %shard_map.50 = (bf16[4,512,512]{2,1,0:T(8,128)(2,1)}, f32[256,512]{1,0:T(8,128)}) custom-call(s32[4]{0:T(128)} %owners_ref.1, bf16[384,1024]{1,0:T(8,128)(2,1)} %x_ref.1, bf16[384,1024]{1,0:T(8,128)(2,1)} %y_ref.1), custom_call_target="tpu_custom_call" | custom-call | tf_op jit(solution)/shard_map/pallas_call | solution.py:408
  77.5 0.0 copy-start
  77.5 3.1 %copy.7 = bf16[4,512,512]{2,1,0:T(8,128)(2,1)} copy(bf16[4,512,512]{2,1,0:T(8,128)(2,1)} %get-tuple-element.4) | data formatting | bytes 4194304
  80.6 0.0 copy-done
  80.6 0.8 copy.8
Async XLA Ops:
  77.5 3.1 %copy-start = (f32[256,512]{1,0:T(8,128)S(1)}, f32[256,512]{1,0:T(8,128)}, u32[]{:S(2)}) copy-start(f32[256,512]{1,0:T(8,128)} %get-tuple-element.5) | copy-start | bytes 1572868
